TPU v7x, 32 devices: a whole 2x2x4 slice. The times are simulated.
32 devices in a mesh: bed: 8 (over y, x, core), layer: 4 (over z).
Axes of the slice: x: 2, y: 2, z: 4, core: 2. Of those that a mesh axis runs over, the one named last changes fastest.
Arguments:
- concentration: float32 [8, 1024, 4096], P('layer', 'bed'), may hold values from 0.2 to 2
- east_velocity: bfloat16 [8, 1024, 4096], P('layer', 'bed'), may hold values from -3 to 3
- north_velocity: bfloat16 [8, 1024, 4096], P('layer', 'bed'), may hold values from -3 to 3
- settling: float32 [1024, 4096], P('bed'), may hold values from 0.02 to 0.15
- surface: float32 [1024, 4096], P('bed'), may hold values from 1.8 to 6
- bed_level: float32 [1024, 4096], P('bed'), may hold values from -1 to 1
- erosion: float32 [1024, 4096], P('bed'), may hold values from 0 to 0.08
- wet_mask: int32 [1024, 4096], P('bed'), may hold values 0 or 1
Outputs:
- new_concentration: float32 [8, 1024, 4096], P('layer', 'bed')
- new_bed: float32 [1024, 4096], P('bed')
Inputs may be any that keep to these rules, and one draw needn't show every extreme that they name: `wet_mask`: 1 marks a wet cell, 0 a dry one.
All inputs are finite; a program needn't handle non-finite values. No bound on the sum of `wet_mask` on one device may be relied on, other than what follows from the above.
Results may differ from a plain program's by a relative error of at most 0.0003.
Values sent between devices are 32-bit elements; how exact they have to be, the bound alone decides.
A program may use at most 128 MiB of HBM per device.

v0:
```python
import jax
import jax.numpy as jnp
from jax import lax
from jax.sharding import PartitionSpec as P

SWEEPS = 4
ADVECT_RATE = 0.1
FLUX_GAIN = 0.15
POROSITY_GAIN = 1.0 / 0.6
RELAX_RATE = 0.2
CRIT_SLOPE = 0.5
DEPTH_FLOOR = 1.0


def padded(block, sides, width):
    for axis, dim in sides:
        count = lax.axis_size(axis)
        forward = [(i, i + 1) for i in range(count - 1)]
        backward = [(target, source) for source, target in forward]
        low = lax.ppermute(
            lax.slice_in_dim(block, block.shape[dim] - width, None, axis=dim), axis, forward
        )
        high = lax.ppermute(lax.slice_in_dim(block, 0, width, axis=dim), axis, backward)
        block = jnp.concatenate([low, block, high], axis=dim)
    return block


def passed_along(block, axis, distance):
    devices = range(lax.axis_size(axis))
    route = [(i - distance, i) for i in devices if i - distance in devices]
    return lax.ppermute(block, axis, route)


def face_divergence(values, speeds, which_axis):
    length_here = values.shape[which_axis]
    left_val = lax.slice_in_dim(values, 0, length_here - 1, axis=which_axis)
    right_val = lax.slice_in_dim(values, 1, length_here, axis=which_axis)
    left_spd = lax.slice_in_dim(speeds, 0, length_here - 1, axis=which_axis)
    right_spd = lax.slice_in_dim(speeds, 1, length_here, axis=which_axis)
    face_speed = 0.5 * (left_spd + right_spd)
    face_flux = jnp.maximum(face_speed, 0.0) * left_val + jnp.minimum(face_speed, 0.0) * right_val
    return lax.slice_in_dim(face_flux, 1, length_here - 1, axis=which_axis) - lax.slice_in_dim(
        face_flux, 0, length_here - 2, axis=which_axis
    )


def slide_sweep(height, wetness):
    drop_x = height[:-1, :] - height[1:, :]
    move_x = (
        RELAX_RATE
        * (drop_x - jnp.clip(drop_x, -CRIT_SLOPE, CRIT_SLOPE))
        * wetness[:-1, :]
        * wetness[1:, :]
    )
    drop_y = height[:, :-1] - height[:, 1:]
    move_y = (
        RELAX_RATE
        * (drop_y - jnp.clip(drop_y, -CRIT_SLOPE, CRIT_SLOPE))
        * wetness[:, :-1]
        * wetness[:, 1:]
    )
    return (
        height[1:-1, 1:-1]
        - move_x[1:, 1:-1]
        + move_x[:-1, 1:-1]
        - move_y[1:-1, 1:]
        + move_y[1:-1, :-1]
    )


def edge_pair(field):
    return jnp.concatenate([field[:, :1], field[:, -1:]], 1)


def body(
    concentration, east_velocity, north_velocity, settling, surface, bed_level, erosion, wet_mask
):
    layers_here = concentration.shape[0]
    layer_count = layers_here * lax.axis_size("layer")
    layer_index = lax.axis_index("layer")
    water_depth = surface - bed_level
    layer_thick = water_depth / layer_count
    east_speed = east_velocity.astype(jnp.float32)
    north_speed = north_velocity.astype(jnp.float32)
    flux_east = east_speed * concentration * layer_thick
    flux_north = north_speed * concentration * layer_thick
    edges = jnp.stack([edge_pair(concentration), edge_pair(east_speed), edge_pair(flux_east)])
    rims = padded(edges, (("bed", 2),), 1)
    before = rims[:, :, :1]
    after = rims[:, :, 3:]
    conc_along = jnp.concatenate([before[0], concentration, after[0]], 1)
    speed_along = jnp.concatenate([before[1], east_speed, after[1]], 1)
    east_wide = jnp.concatenate([before[2], flux_east, after[2]], 1)
    upper_row = passed_along(concentration[0], "layer", -1)
    pad_y = ((0, 0), (0, 0), (1, 1))
    advect = face_divergence(conc_along, speed_along, 1) + face_divergence(
        jnp.pad(concentration, pad_y), jnp.pad(north_speed, pad_y), 2
    )
    bottom_flag = (layer_index == 0).astype(jnp.float32)
    falling = jnp.concatenate([concentration[1:], upper_row[None]], 0) * settling
    source = falling - settling * concentration
    source = source.at[0].add(bottom_flag * erosion)
    settled = concentration - ADVECT_RATE * advect + layer_count / water_depth * source
    north_wide = jnp.pad(flux_north, pad_y)
    spread = 0.5 * (
        east_wide[:, 2:, :] - east_wide[:, :-2, :] + north_wide[:, :, 2:] - north_wide[:, :, :-2]
    )
    bed_change = FLUX_GAIN * jnp.sum(spread, 0) - bottom_flag * settling * concentration[0]
    wet_float = wet_mask.astype(jnp.float32)
    rim_width, rounds = (1, SWEEPS)
    summed_flux = lax.psum(bed_change, "layer")
    height = bed_level - POROSITY_GAIN * wet_float * (summed_flux + erosion)
    side_pad = ((0, 0), (rim_width, rim_width))
    wet_wide = jnp.pad(padded(wet_float, (("bed", 0),), rim_width), side_pad)
    for round_index in range(rounds):
        height_wide = jnp.pad(padded(height, (("bed", 0),), rim_width), side_pad)
        wetness = wet_wide
        height_wide = slide_sweep(height_wide, wetness)
        wetness = wetness[1:-1, 1:-1]
        height = height_wide
    new_depth = jnp.maximum(surface - height, DEPTH_FLOOR)
    return (settled * (water_depth / new_depth), height)


def solution(mesh):
    in_specs = (
        P("layer", "bed", None),
        P("layer", "bed", None),
        P("layer", "bed", None),
        P("bed", None),
        P("bed", None),
        P("bed", None),
        P("bed", None),
        P("bed", None),
    )
    out_specs = (P("layer", "bed", None), P("bed", None))
    return jax.shard_map(body, mesh=mesh, in_specs=in_specs, out_specs=out_specs, check_vma=False)
```

profile of v0, /device:TPU:4, one launch (start us, length us, event | category | flops | bytes accessed | tf_op | source)
XLA Modules:
  0.0 256.3 jit_solution(9465956623220491633)
XLA Ops:
  7.2 2.7 %fusion.39 = (f32[1,128,4096]{2,1,0:T(8,128)S(1)}, f32[128,4096]{1,0:T(8,128)S(1)}) fusion(f32[2,128,4096]{2,1,0:T(8,128)} %param.10), kind=kLoop, calls=%fused_computation.111 | loop fusion | bytes 8388608 | tf_op jit(solution)/shard_map/slice | solution.py:100
  11.9 3.4 %broadcast_divide_fusion = (f32[128,4096]{1,0:T(8,128)}, f32[128,4096]{1,0:T(8,128)S(1)}) fusion(f32[128,4096]{1,0:T(8,128)} %param.14, f32[128,4096]{1,0:T(8,128)S(1)} %copy-done.16), kind=kLoop, calls=%fused_computation.99 | loop fusion | flops 1048576 | bytes 8388608 | tf_op jit(solution)/shard_map/div | solution.py:103
  16.8 42.6 %collective-permute-done.2 = f32[128,4096]{1,0:T(8,128)S(1)} collective-permute-done((f32[128,4096]{1,0:T(8,128)S(1)}, f32[128,4096]{1,0:T(8,128)S(1)}, u32[]{:S(2)}, u32[]{:S(2)}) %collective-permute-start.2) | collective-permute-done | bytes 2097184 | tf_op jit(solution)/shard_map/ppermute | solution.py:31
  59.5 4.4 %multiply_multiply_fusion = (f32[2,128,4096]{2,1,0:T(8,128)}, f32[2,128,4096]{2,1,0:T(8,128)S(1)}, f32[2,128,4096]{2,1,0:T(8,128)}) fusion(f32[2,128,4096]{2,1,0:T(8,128)S(1)} %copy-done, f32[128,4096]{1,0:T(8,128)S(1)} %broadcast_multiply_fusion, bf16[2,128,4096]{2,1,0:T(8,128)(2,1)S(1)} %copy-done.11, bf16[2,128,4096]{2,1,0:T(8,128)(2,1)S(1)} %copy-done.8, ...), kind=kLoop, calls=%fused_computation.22 | loop fusion | flops 10485760 | bytes 29360128 | tf_op jit(solution)/shard_map/mul | solution.py:86
  68.2 2.4 collective-permute-start
  70.7 4.4 %collective-permute-done = f32[3,2,1,4096]{3,2,1,0:T(1,128)S(1)} collective-permute-done((f32[3,2,1,4096]{3,2,1,0:T(1,128)S(1)}, f32[3,2,1,4096]{3,2,1,0:T(1,128)S(1)}, u32[]{:S(2)}, u32[]{:S(2)}) %collective-permute-start) | collective-permute-done | bytes 98336 | tf_op jit(solution)/shard_map/ppermute | solution.py:20
  75.1 8.3 %fusion.6 = f32[128,4096]{1,0:T(8,128)S(1)} fusion(f32[2,128,4096]{2,1,0:T(8,128)} %copy-done.6, f32[2,1,4096]{2,1,0:T(1,128)S(1)} %get-tuple-element.44, f32[2,1,4096]{2,1,0:T(1,128)S(1)} %get-tuple-element.41, f32[2,128,4096]{2,1,0:T(8,128)} %get-tuple-element.18), kind=kLoop, calls=%fused_computation.11 | loop fusion | flops 6815744 | bytes 10551296 | tf_op jit(solution)/shard_map/reduce_sum | solution.py:108
  90.6 4.5 %collective-permute-start.6 = (f32[1,4096]{1,0:T(1,128)S(1)}, f32[1,4096]{1,0:T(1,128)S(1)}, u32[]{:S(2)}, u32[]{:S(2)}) collective-permute-start(f32[1,4096]{1,0:T(1,128)S(1)} %get-tuple-element.34), channel_id=1, source_target_pairs={{4,0},{8,4},{12,8},{16,12},{20,16},{24,20},{28,24},{5,1},{9,5},{13... | collective-permute-start | bytes 49160 | tf_op jit(solution)/shard_map/ppermute | solution.py:23
  95.1 2.5 convert_element_type.23
  97.6 73.6 %all-reduce.10.cloned.1.call-done = f32[128,4096]{1,0:T(8,128)} async-done(((f32[128,4096]{1,0:T(8,128)}), f32[128,4096]{1,0:T(8,128)}) %all-reduce.10.cloned.1.call-update) | async-done | bytes 2097168 | tf_op jit(solution)/shard_map/psum | solution.py:111
  171.2 4.2 %multiply_subtract_fusion = f32[128,4096]{1,0:T(8,128)S(1)} fusion(f32[128,4096]{1,0:T(8,128)} %param.15, f32[128,4096]{1,0:T(8,128)} %all-reduce.10.cloned.1.call-done, f32[128,4096]{1,0:T(8,128)} %param.16, s32[128,4096]{1,0:T(8,128)} %param.17), kind=kLoop, calls=%fused_computation.96 | loop fusion | flops 2621440 | bytes 10485760 | tf_op jit(solution)/shard_map/sub | solution.py:112
  177.4 4.5 %collective-permute-start.4 = (f32[1,4096]{1,0:T(1,128)S(1)}, f32[1,4096]{1,0:T(1,128)S(1)}, u32[]{:S(2)}, u32[]{:S(2)}) collective-permute-start(f32[1,4096]{1,0:T(1,128)S(1)} %get-tuple-element.36), channel_id=1, source_target_pairs={{4,0},{8,4},{12,8},{16,12},{20,16},{24,20},{28,24},{5,1},{9,5},{13... | collective-permute-start | bytes 49160 | tf_op jit(solution)/shard_map/ppermute | solution.py:23
  188.0 2.7 %collective-permute-start.7 = (f32[1,4096]{1,0:T(1,128)S(1)}, f32[1,4096]{1,0:T(1,128)S(1)}, u32[]{:S(2)}, u32[]{:S(2)}) collective-permute-start(f32[1,4096]{1,0:T(1,128)S(1)} %get-tuple-element.31), channel_id=1, source_target_pairs={{0,4},{4,8},{8,12},{12,16},{16,20},{20,24},{24,28},{1,5},{5,9},{9,... | collective-permute-start | bytes 49160 | tf_op jit(solution)/shard_map/ppermute | solution.py:20
  190.8 4.1 %collective-permute-start.8 = (f32[1,4096]{1,0:T(1,128)S(1)}, f32[1,4096]{1,0:T(1,128)S(1)}, u32[]{:S(2)}, u32[]{:S(2)}) collective-permute-start(f32[1,4096]{1,0:T(1,128)S(1)} %get-tuple-element.32), channel_id=1, source_target_pairs={{4,0},{8,4},{12,8},{16,12},{20,16},{24,20},{28,24},{5,1},{9,5},{13... | collective-permute-start | bytes 49160 | tf_op jit(solution)/shard_map/ppermute | solution.py:23
  194.9 2.4 multiply_add_fusion
  197.3 2.5 convert_element_type.22
  204.4 2.4 collective-permute-start.10
  209.4 3.4 %collective-permute-done.9 = f32[1,4096]{1,0:T(1,128)S(1)} collective-permute-done((f32[1,4096]{1,0:T(1,128)S(1)}, f32[1,4096]{1,0:T(1,128)S(1)}, u32[]{:S(2)}, u32[]{:S(2)}) %collective-permute-start.9) | collective-permute-done | bytes 16416 | tf_op jit(solution)/shard_map/ppermute | solution.py:20
  219.4 4.8 %collective-permute-start.12 = (f32[1,4096]{1,0:T(1,128)S(1)}, f32[1,4096]{1,0:T(1,128)S(1)}, u32[]{:S(2)}, u32[]{:S(2)}) collective-permute-start(f32[1,4096]{1,0:T(1,128)S(1)} %get-tuple-element.28), channel_id=1, source_target_pairs={{4,0},{8,4},{12,8},{16,12},{20,16},{24,20},{28,24},{5,1},{9,5},{13... | collective-permute-start | bytes 49160 | tf_op jit(solution)/shard_map/ppermute | solution.py:23
  224.2 5.1 %fusion.1 = f32[2,129,4096]{2,1,0:T(8,128)S(1)} fusion(f32[2,128,4096]{2,1,0:T(8,128)S(1)} %copy-done.2, f32[2,1,4096]{2,1,0:T(1,128)S(1)} %get-tuple-element.45, f32[2,1,4096]{2,1,0:T(1,128)S(1)} %get-tuple-element.42, f32[2,1,4096]{2,1,0:T(1,128)S(1)} %get-tuple-element.43, f32[2,128,4096]{2,1,0:T(8,128)} %convert_element_type.22, ...), kind=kLoop, calls=%fused_computation.3 | loop fusion | flops 11624448 | bytes 12746752 | tf_op jit(solution)/shard_map/add | solution.py:41
  230.0 2.2 fusion.33
  232.2 2.6 %fusion.36 = f32[130,4097]{1,0:T(8,128)} fusion(f32[130,4098]{1,0:T(8,128)S(1)} %select_maximum_fusion, f32[130,4098]{1,0:T(8,128)S(1)} %select_maximum_fusion.6), kind=kLoop, calls=%fused_computation.57 | loop fusion | flops 3195660 | bytes 10652200 | tf_op jit(solution)/shard_map/mul | solution.py:57
  234.9 9.2 %maximum_divide_fusion = (f32[128,4096]{1,0:T(8,128)}, f32[128,4096]{1,0:T(8,128)}) fusion(f32[128,4096]{1,0:T(8,128)} %copy-done.5, f32[128,4096]{1,0:T(8,128)} %param.14, f32[130,4097]{1,0:T(8,128)} %fusion.36, f32[129,4098]{1,0:T(8,128)} %fusion.33, f32[128,4096]{1,0:T(8,128)} %copy-done.4), kind=kLoop, calls=%fused_computation.95 | loop fusion | flops 3670016 | bytes 18874368 | tf_op jit(solution)/shard_map/div | solution.py:122
  244.0 5.4 %fusion.11 = f32[2,128,4096]{2,1,0:T(8,128)} fusion(f32[2,128,4096]{2,1,0:T(8,128)S(1)} %copy-done.2, f32[2,128,4097]{2,1,0:T(8,128)S(1)} %multiply_add_fusion, f32[2,129,4096]{2,1,0:T(8,128)S(1)} %fusion.1, f32[2,128,4096]{2,1,0:T(8,128)S(1)} %fusion.38, f32[128,4096]{1,0:T(8,128)} %get-tuple-element.16, f32[128,4096]{1,0:T(8,128)} %get-tuple-element.14), kind=kLoop, calls=%fused_computation.18 | loop fusion | flops 8388608 | bytes 33554432 | tf_op jit(solution)/shard_map/mul | solution.py:122
  (84 shorter events, 37.4 us)
Async XLA Ops:
  7.2 164.1 %all-reduce.10.cloned.1.call-start = ((), (), s32[]{:S(2)}) async-start(), calls=%async_computation | async-start | bytes 4194304 | tf_op jit(solution)/shard_map/psum | solution.py:111
  9.9 49.5 %collective-permute-start.2 = (f32[128,4096]{1,0:T(8,128)S(1)}, f32[128,4096]{1,0:T(8,128)S(1)}, u32[]{:S(2)}, u32[]{:S(2)}) collective-permute-start(f32[128,4096]{1,0:T(8,128)S(1)} %get-tuple-element.22), channel_id=1, source_target_pairs={{1,0},{2,1},{3,2},{5,4},{6,5},{7,6},{9,8},{10,9},{11,10},{13,12},{... | collective-permute-start | bytes 6291464 | tf_op jit(solution)/shard_map/ppermute | solution.py:31
  15.3 44.2 %copy-start.11 = (bf16[2,128,4096]{2,1,0:T(8,128)(2,1)S(1)}, bf16[2,128,4096]{2,1,0:T(8,128)(2,1)}, u32[]{:S(2)}) copy-start(bf16[2,128,4096]{2,1,0:T(8,128)(2,1)} %param.12) | copy-start | bytes 6291460
  15.3 44.2 %copy-start.13 = (f32[128,4096]{1,0:T(8,128)S(1)}, f32[128,4096]{1,0:T(8,128)}, u32[]{:S(2)}) copy-start(f32[128,4096]{1,0:T(8,128)} %param.13) | copy-start | bytes 6291460
  66.3 4.4 %collective-permute-start.1 = (f32[3,2,1,4096]{3,2,1,0:T(1,128)S(1)}, f32[3,2,1,4096]{3,2,1,0:T(1,128)S(1)}, u32[]{:S(2)}, u32[]{:S(2)}) collective-permute-start(f32[3,2,1,4096]{3,2,1,0:T(1,128)S(1)} %get-tuple-element.39), channel_id=1, source_target_pairs={{4,0},{8,4},{12,8},{16,12},{20,16},{24,20},{28,24},{5,1},{9,5},{13... | collective-permute-start | bytes 294920 | tf_op jit(solution)/shard_map/ppermute | solution.py:23
  68.2 6.8 %collective-permute-start = (f32[3,2,1,4096]{3,2,1,0:T(1,128)S(1)}, f32[3,2,1,4096]{3,2,1,0:T(1,128)S(1)}, u32[]{:S(2)}, u32[]{:S(2)}) collective-permute-start(f32[3,2,1,4096]{3,2,1,0:T(1,128)S(1)} %get-tuple-element.40), channel_id=1, source_target_pairs={{0,4},{4,8},{8,12},{12,16},{16,20},{20,24},{24,28},{1,5},{5,9},{9,... | collective-permute-start | bytes 294920 | tf_op jit(solution)/shard_map/ppermute | solution.py:20
  75.1 8.3 %copy-start.1 = (f32[2,128,4096]{2,1,0:T(8,128)S(1)}, f32[2,128,4096]{2,1,0:T(8,128)}, u32[]{:S(2)}) copy-start(f32[2,128,4096]{2,1,0:T(8,128)} %param.10) | copy-start | bytes 12582916
  75.1 8.3 %copy-start.14 = (f32[128,4096]{1,0:T(8,128)S(1)}, f32[128,4096]{1,0:T(8,128)}, u32[]{:S(2)}) copy-start(f32[128,4096]{1,0:T(8,128)} %param.13) | copy-start | bytes 6291460
  85.3 9.8 %copy-start.12 = (bf16[2,128,4096]{2,1,0:T(8,128)(2,1)S(1)}, bf16[2,128,4096]{2,1,0:T(8,128)(2,1)}, u32[]{:S(2)}) copy-start(bf16[2,128,4096]{2,1,0:T(8,128)(2,1)} %param.12) | copy-start | bytes 6291460
  88.6 93.3 %collective-permute-start.5 = (f32[1,4096]{1,0:T(1,128)S(1)}, f32[1,4096]{1,0:T(1,128)S(1)}, u32[]{:S(2)}, u32[]{:S(2)}) collective-permute-start(f32[1,4096]{1,0:T(1,128)S(1)} %get-tuple-element.33), channel_id=1, source_target_pairs={{0,4},{4,8},{8,12},{12,16},{16,20},{20,24},{24,28},{1,5},{5,9},{9,... | collective-permute-start | bytes 49160 | tf_op jit(solution)/shard_map/ppermute | solution.py:20
  90.6 91.4 %collective-permute-start.6 = (f32[1,4096]{1,0:T(1,128)S(1)}, f32[1,4096]{1,0:T(1,128)S(1)}, u32[]{:S(2)}, u32[]{:S(2)}) collective-permute-start(f32[1,4096]{1,0:T(1,128)S(1)} %get-tuple-element.34), channel_id=1, source_target_pairs={{4,0},{8,4},{12,8},{16,12},{20,16},{24,20},{28,24},{5,1},{9,5},{13... | collective-permute-start | bytes 49160 | tf_op jit(solution)/shard_map/ppermute | solution.py:23
  171.2 10.7 %copy-start.10 = (f32[128,4096]{1,0:T(8,128)S(1)}, f32[128,4096]{1,0:T(8,128)}, u32[]{:S(2)}) copy-start(f32[128,4096]{1,0:T(8,128)} %copy-done.9) | copy-start | bytes 6291460
  175.5 7.2 %collective-permute-start.3 = (f32[1,4096]{1,0:T(1,128)S(1)}, f32[1,4096]{1,0:T(1,128)S(1)}, u32[]{:S(2)}, u32[]{:S(2)}) collective-permute-start(f32[1,4096]{1,0:T(1,128)S(1)} %get-tuple-element.35), channel_id=1, source_target_pairs={{0,4},{4,8},{8,12},{12,16},{16,20},{20,24},{24,28},{1,5},{5,9},{9,... | collective-permute-start | bytes 49160 | tf_op jit(solution)/shard_map/ppermute | solution.py:20
  177.4 6.0 %collective-permute-start.4 = (f32[1,4096]{1,0:T(1,128)S(1)}, f32[1,4096]{1,0:T(1,128)S(1)}, u32[]{:S(2)}, u32[]{:S(2)}) collective-permute-start(f32[1,4096]{1,0:T(1,128)S(1)} %get-tuple-element.36), channel_id=1, source_target_pairs={{4,0},{8,4},{12,8},{16,12},{20,16},{24,20},{28,24},{5,1},{9,5},{13... | collective-permute-start | bytes 49160 | tf_op jit(solution)/shard_map/ppermute | solution.py:23
  186.2 8.7 %copy-start.2 = (f32[2,128,4096]{2,1,0:T(8,128)S(1)}, f32[2,128,4096]{2,1,0:T(8,128)}, u32[]{:S(2)}) copy-start(f32[2,128,4096]{2,1,0:T(8,128)} %param.10) | copy-start | bytes 12582916
  186.2 8.7 %copy-start.7 = (f32[2,128,4096]{2,1,0:T(8,128)S(1)}, f32[2,128,4096]{2,1,0:T(8,128)}, u32[]{:S(2)}) copy-start(f32[2,128,4096]{2,1,0:T(8,128)} %convert_element_type.23) | copy-start | bytes 12582916
  188.0 11.7 %collective-permute-start.7 = (f32[1,4096]{1,0:T(1,128)S(1)}, f32[1,4096]{1,0:T(1,128)S(1)}, u32[]{:S(2)}, u32[]{:S(2)}) collective-permute-start(f32[1,4096]{1,0:T(1,128)S(1)} %get-tuple-element.31), channel_id=1, source_target_pairs={{0,4},{4,8},{8,12},{12,16},{16,20},{20,24},{24,28},{1,5},{5,9},{9,... | collective-permute-start | bytes 49160 | tf_op jit(solution)/shard_map/ppermute | solution.py:20
  190.8 9.0 %collective-permute-start.8 = (f32[1,4096]{1,0:T(1,128)S(1)}, f32[1,4096]{1,0:T(1,128)S(1)}, u32[]{:S(2)}, u32[]{:S(2)}) collective-permute-start(f32[1,4096]{1,0:T(1,128)S(1)} %get-tuple-element.32), channel_id=1, source_target_pairs={{4,0},{8,4},{12,8},{16,12},{20,16},{24,20},{28,24},{5,1},{9,5},{13... | collective-permute-start | bytes 49160 | tf_op jit(solution)/shard_map/ppermute | solution.py:23
  202.6 6.2 %copy-start.3 = (f32[2,128,4096]{2,1,0:T(8,128)S(1)}, f32[2,128,4096]{2,1,0:T(8,128)}, u32[]{:S(2)}) copy-start(f32[2,128,4096]{2,1,0:T(8,128)} %get-tuple-element.20) | copy-start | bytes 12582916
  204.4 5.0 %collective-permute-start.10 = (f32[1,4096]{1,0:T(1,128)S(1)}, f32[1,4096]{1,0:T(1,128)S(1)}, u32[]{:S(2)}, u32[]{:S(2)}) collective-permute-start(f32[1,4096]{1,0:T(1,128)S(1)} %get-tuple-element.30), channel_id=1, source_target_pairs={{4,0},{8,4},{12,8},{16,12},{20,16},{24,20},{28,24},{5,1},{9,5},{13... | collective-permute-start | bytes 49160 | tf_op jit(solution)/shard_map/ppermute | solution.py:23
  206.8 6.0 %collective-permute-start.9 = (f32[1,4096]{1,0:T(1,128)S(1)}, f32[1,4096]{1,0:T(1,128)S(1)}, u32[]{:S(2)}, u32[]{:S(2)}) collective-permute-start(f32[1,4096]{1,0:T(1,128)S(1)} %get-tuple-element.29), channel_id=1, source_target_pairs={{0,4},{4,8},{8,12},{12,16},{16,20},{20,24},{24,28},{1,5},{5,9},{9,... | collective-permute-start | bytes 49160 | tf_op jit(solution)/shard_map/ppermute | solution.py:20
  217.4 11.9 %copy-start.4 = (f32[128,4096]{1,0:T(8,128)}, f32[128,4096]{1,0:T(8,128)S(1)}, u32[]{:S(2)}) copy-start(f32[128,4096]{1,0:T(8,128)S(1)} %slice_add_fusion.2) | copy-start | bytes 6291460
  217.5 11.8 %collective-permute-start.11 = (f32[1,4096]{1,0:T(1,128)S(1)}, f32[1,4096]{1,0:T(1,128)S(1)}, u32[]{:S(2)}, u32[]{:S(2)}) collective-permute-start(f32[1,4096]{1,0:T(1,128)S(1)} %get-tuple-element.27), channel_id=1, source_target_pairs={{0,4},{4,8},{8,12},{12,16},{16,20},{20,24},{24,28},{1,5},{5,9},{9,... | collective-permute-start | bytes 49160 | tf_op jit(solution)/shard_map/ppermute | solution.py:20
  219.4 9.9 %collective-permute-start.12 = (f32[1,4096]{1,0:T(1,128)S(1)}, f32[1,4096]{1,0:T(1,128)S(1)}, u32[]{:S(2)}, u32[]{:S(2)}) collective-permute-start(f32[1,4096]{1,0:T(1,128)S(1)} %get-tuple-element.28), channel_id=1, source_target_pairs={{4,0},{8,4},{12,8},{16,12},{20,16},{24,20},{28,24},{5,1},{9,5},{13... | collective-permute-start | bytes 49160 | tf_op jit(solution)/shard_map/ppermute | solution.py:23
  (7 other events, 24.3 us)
Sparse Core Ops, SparseCore 0:
  85.4 85.7 all-reduce.9
where the time goes:
time: 257 us; the launch traced here: 256 us
  waiting for transfers between devices  125 us (49%)
  other arithmetic  72.3 us (28%)
  starting transfers between devices  36.6 us (14%)
  between operations  14.6 us (6%)
  local copies, waits for them, and re-layouts  8.08 us (3%)
    psum x1, waiting for transfers between devices, body(): summed_flux = lax.psum(bed_change, 'layer')  73.6 us
    ppermute x1, waiting for transfers between devices, passed_along(): return lax.ppermute(block, axis, route)  42.6 us
    ppermute x6, starting transfers between devices, padded(): lax.ppermute(lax.slice_in_dim(block, 0, width, axis=dim), axis, backward)  22.2 us
    ppermute x6, starting transfers between devices, padded(): lax.ppermute(lax.slice_in_dim(block, block.shape[dim] - width, None, axis...  12.8 us
    div x1, other arithmetic, body(): return (settled * (water_depth / new_depth), height)  9.16 us
    reduce_sum x1, other arithmetic, body(): jnp.sum(spread, 0)  8.31 us
    ppermute x6, waiting for transfers between devices, padded(): lax.ppermute(lax.slice_in_dim(block, block.shape[dim] - width, None, axis...  7.76 us
    add x2, other arithmetic, face_divergence(): jnp.maximum(face_speed, 0.0) * left_val  7.51 us
  transfers between devices with their start and end apart: 14, of which 5 were waited for; matrix products, arithmetic and copies ran while one was open for 9% of the time, Pallas kernels for 0%

commit v1 on v0

--- a/solution.py
+++ b/solution.py
@@ -108,7 +108,11 @@
     bed_change = FLUX_GAIN * jnp.sum(spread, 0) - bottom_flag * settling * concentration[0]
     wet_float = wet_mask.astype(jnp.float32)
     rim_width, rounds = (1, SWEEPS)
-    summed_flux = lax.psum(bed_change, "layer")
+    summed_flux = bed_change
+    for hop in (1, 2):
+        summed_flux = summed_flux + lax.ppermute(
+            summed_flux, "layer", [(dev, dev ^ hop) for dev in range(4)]
+        )
     height = bed_level - POROSITY_GAIN * wet_float * (summed_flux + erosion)
     side_pad = ((0, 0), (rim_width, rim_width))
     wet_wide = jnp.pad(padded(wet_float, (("bed", 0),), rim_width), side_pad)

time: 257 us -> 289 us (1.12)
  waiting for transfers between devices: 125 us -> 173 us
  between operations: 14.6 us -> 1.21 us
  other arithmetic: 72.3 us -> 65.4 us
  starting transfers between devices: 36.6 us -> 43.1 us
    ppermute x0 -> x2, waiting for transfers between devices: none -> 125 us  [body(): lax.ppermute(summed_flux, 'layer', [(dev, dev ^ hop) for dev in range(4)])]
    psum x1 -> x0, waiting for transfers between devices: 73.6 us -> none  [body(): summed_flux = lax.psum(bed_change, 'layer')]
    ppermute x0 -> x2, starting transfers between devices: none -> 4.3 us  [body(): lax.ppermute(summed_flux, 'layer', [(dev, dev ^ hop) for dev in range(4)])]
    ppermute x6, starting transfers between devices: 22.2 us -> 25.3 us  [padded(): lax.ppermute(lax.slice_in_dim(block, 0, width, axis=dim), axis, backward)]
  transfers between devices with their start and end apart: 14 -> 15, of which waited for: 5 -> 6; matrix products, arithmetic and copies ran while one was open for 9% -> 6% of each run, Pallas kernels for 0% -> 0%
where the time goes in v1:
time: 289 us; the launch traced here: 288 us
  waiting for transfers between devices  173 us (60%)
  other arithmetic  65.4 us (23%)
  starting transfers between devices  43.1 us (15%)
  local copies, waits for them, and re-layouts  5.43 us (2%)
    ppermute x2, waiting for transfers between devices, body(): lax.ppermute(summed_flux, 'layer', [(dev, dev ^ hop) for dev in range(4)])  125 us
    ppermute x1, waiting for transfers between devices, passed_along(): return lax.ppermute(block, axis, route)  41.5 us
    ppermute x6, starting transfers between devices, padded(): lax.ppermute(lax.slice_in_dim(block, 0, width, axis=dim), axis, backward)  25.3 us
    ppermute x6, starting transfers between devices, padded(): lax.ppermute(lax.slice_in_dim(block, block.shape[dim] - width, None, axis...  12 us
    div x1, other arithmetic, body(): return (settled * (water_depth / new_depth), height)  9.17 us
    reduce_sum x1, other arithmetic, body(): jnp.sum(spread, 0)  8.5 us
    mul x4, other arithmetic, slide_sweep(): RELAX_RATE * (drop_y - jnp.clip(drop_y, -CRIT_SLOPE, CRIT_SLOPE))  6.43 us
  transfers between devices with their start and end apart: 15, of which 6 were waited for; matrix products, arithmetic and copies ran while one was open for 6% of the time, Pallas kernels for 0%

profile of v1, /device:TPU:4, one launch (start us, length us, event | category | flops | bytes accessed | tf_op | source)
XLA Modules:
  0.0 287.7 jit_solution(9026833961868159535)
XLA Ops:
  0.7 2.7 fusion.39
  5.4 4.0 %broadcast_divide_fusion = (f32[128,4096]{1,0:T(8,128)}, f32[128,4096]{1,0:T(8,128)}) fusion(f32[128,4096]{1,0:T(8,128)S(1)} %copy-done.11, f32[128,4096]{1,0:T(8,128)} %param.15), kind=kLoop, calls=%fused_computation.99 | loop fusion | flops 1048576 | bytes 8388608 | tf_op jit(solution)/shard_map/div | solution.py:103
  11.3 41.5 %collective-permute-done.2 = f32[128,4096]{1,0:T(8,128)S(1)} collective-permute-done((f32[128,4096]{1,0:T(8,128)S(1)}, f32[128,4096]{1,0:T(8,128)S(1)}, u32[]{:S(2)}, u32[]{:S(2)}) %collective-permute-start.2) | collective-permute-done | bytes 2097184 | tf_op jit(solution)/shard_map/ppermute | solution.py:31
  52.9 4.4 %multiply_multiply_fusion = (f32[2,128,4096]{2,1,0:T(8,128)}, f32[2,128,4096]{2,1,0:T(8,128)S(1)}, f32[2,128,4096]{2,1,0:T(8,128)}) fusion(f32[2,128,4096]{2,1,0:T(8,128)S(1)} %copy-done, f32[128,4096]{1,0:T(8,128)S(1)} %broadcast_multiply_fusion, bf16[2,128,4096]{2,1,0:T(8,128)(2,1)S(1)} %copy-done.6, bf16[2,128,4096]{2,1,0:T(8,128)(2,1)S(1)} %copy-done.5, ...), kind=kLoop, calls=%fused_computation.22 | loop fusion | flops 10485760 | bytes 29360128 | tf_op jit(solution)/shard_map/mul | solution.py:86
  57.3 2.0 copy-done.4
  61.6 2.4 collective-permute-start
  64.1 4.4 %collective-permute-done = f32[3,2,1,4096]{3,2,1,0:T(1,128)S(1)} collective-permute-done((f32[3,2,1,4096]{3,2,1,0:T(1,128)S(1)}, f32[3,2,1,4096]{3,2,1,0:T(1,128)S(1)}, u32[]{:S(2)}, u32[]{:S(2)}) %collective-permute-start) | collective-permute-done | bytes 98336 | tf_op jit(solution)/shard_map/ppermute | solution.py:20
  68.5 8.5 %fusion.6 = f32[128,4096]{1,0:T(8,128)S(1)} fusion(f32[2,128,4096]{2,1,0:T(8,128)} %copy-done.4, f32[2,1,4096]{2,1,0:T(1,128)S(1)} %get-tuple-element.44, f32[2,1,4096]{2,1,0:T(1,128)S(1)} %get-tuple-element.41, f32[2,128,4096]{2,1,0:T(8,128)} %get-tuple-element.18), kind=kLoop, calls=%fused_computation.11 | loop fusion | flops 6815744 | bytes 10551296 | tf_op jit(solution)/shard_map/reduce_sum | solution.py:108
  79.2 44.3 %collective-permute-done.3 = f32[128,4096]{1,0:T(8,128)S(1)} collective-permute-done((f32[128,4096]{1,0:T(8,128)S(1)}, f32[128,4096]{1,0:T(8,128)S(1)}, u32[]{:S(2)}, u32[]{:S(2)}) %collective-permute-start.3) | collective-permute-done | bytes 2097184 | tf_op jit(solution)/shard_map/ppermute | solution.py:113
  123.7 2.7 collective-permute-start.4
  128.5 4.8 %collective-permute-start.8 = (f32[1,4096]{1,0:T(1,128)S(1)}, f32[1,4096]{1,0:T(1,128)S(1)}, u32[]{:S(2)}, u32[]{:S(2)}) collective-permute-start(f32[1,4096]{1,0:T(1,128)S(1)} %get-tuple-element.34), channel_id=1, source_target_pairs={{4,0},{8,4},{12,8},{16,12},{20,16},{24,20},{28,24},{5,1},{9,5},{13... | collective-permute-start | bytes 49160 | tf_op jit(solution)/shard_map/ppermute | solution.py:23
  133.8 80.8 %collective-permute-done.4 = f32[128,4096]{1,0:T(8,128)} collective-permute-done((f32[128,4096]{1,0:T(8,128)S(1)}, f32[128,4096]{1,0:T(8,128)}, u32[]{:S(2)}, u32[]{:S(2)}) %collective-permute-start.4) | collective-permute-done | bytes 2097184 | tf_op jit(solution)/shard_map/ppermute | solution.py:113
  214.6 2.5 multiply_subtract_fusion
  219.1 4.7 %collective-permute-start.6 = (f32[1,4096]{1,0:T(1,128)S(1)}, f32[1,4096]{1,0:T(1,128)S(1)}, u32[]{:S(2)}, u32[]{:S(2)}) collective-permute-start(f32[1,4096]{1,0:T(1,128)S(1)} %get-tuple-element.36), channel_id=1, source_target_pairs={{4,0},{8,4},{12,8},{16,12},{20,16},{24,20},{28,24},{5,1},{9,5},{13... | collective-permute-start | bytes 49160 | tf_op jit(solution)/shard_map/ppermute | solution.py:23
  229.8 4.5 %collective-permute-start.10 = (f32[1,4096]{1,0:T(1,128)S(1)}, f32[1,4096]{1,0:T(1,128)S(1)}, u32[]{:S(2)}, u32[]{:S(2)}) collective-permute-start(f32[1,4096]{1,0:T(1,128)S(1)} %get-tuple-element.32), channel_id=1, source_target_pairs={{4,0},{8,4},{12,8},{16,12},{20,16},{24,20},{28,24},{5,1},{9,5},{13... | collective-permute-start | bytes 49160 | tf_op jit(solution)/shard_map/ppermute | solution.py:23
  236.3 2.4 multiply_add_fusion
  247.0 4.8 %collective-permute-start.12 = (f32[1,4096]{1,0:T(1,128)S(1)}, f32[1,4096]{1,0:T(1,128)S(1)}, u32[]{:S(2)}, u32[]{:S(2)}) collective-permute-start(f32[1,4096]{1,0:T(1,128)S(1)} %get-tuple-element.30), channel_id=1, source_target_pairs={{4,0},{8,4},{12,8},{16,12},{20,16},{24,20},{28,24},{5,1},{9,5},{13... | collective-permute-start | bytes 49160 | tf_op jit(solution)/shard_map/ppermute | solution.py:23
  251.7 2.3 fusion.38
  260.7 4.5 %collective-permute-start.14 = (f32[1,4096]{1,0:T(1,128)S(1)}, f32[1,4096]{1,0:T(1,128)S(1)}, u32[]{:S(2)}, u32[]{:S(2)}) collective-permute-start(f32[1,4096]{1,0:T(1,128)S(1)} %get-tuple-element.28), channel_id=1, source_target_pairs={{4,0},{8,4},{12,8},{16,12},{20,16},{24,20},{28,24},{5,1},{9,5},{13... | collective-permute-start | bytes 49160 | tf_op jit(solution)/shard_map/ppermute | solution.py:23
  265.2 2.3 fusion.1
  268.3 2.2 fusion.33
  270.5 2.6 fusion.36
  273.1 9.2 %maximum_divide_fusion = (f32[128,4096]{1,0:T(8,128)}, f32[128,4096]{1,0:T(8,128)}) fusion(f32[128,4096]{1,0:T(8,128)} %get-tuple-element.15, f32[128,4096]{1,0:T(8,128)} %param.14, f32[130,4097]{1,0:T(8,128)} %fusion.36, f32[129,4098]{1,0:T(8,128)} %fusion.33, f32[128,4096]{1,0:T(8,128)} %copy-done.3), kind=kLoop, calls=%fused_computation.95 | loop fusion | flops 3670016 | bytes 18874368 | tf_op jit(solution)/shard_map/div | solution.py:126
  282.3 5.4 %fusion.11 = f32[2,128,4096]{2,1,0:T(8,128)} fusion(f32[2,128,4096]{2,1,0:T(8,128)S(1)} %copy-done.1, f32[2,128,4097]{2,1,0:T(8,128)S(1)} %multiply_add_fusion, f32[2,129,4096]{2,1,0:T(8,128)S(1)} %fusion.1, f32[2,128,4096]{2,1,0:T(8,128)S(1)} %fusion.38, f32[128,4096]{1,0:T(8,128)} %get-tuple-element.16, f32[128,4096]{1,0:T(8,128)} %get-tuple-element.14), kind=kLoop, calls=%fused_computation.18 | loop fusion | flops 8388608 | bytes 33554432 | tf_op jit(solution)/shard_map/mul | solution.py:126
  (80 shorter events, 36.6 us)
Async XLA Ops:
  3.3 49.5 %collective-permute-start.2 = (f32[128,4096]{1,0:T(8,128)S(1)}, f32[128,4096]{1,0:T(8,128)S(1)}, u32[]{:S(2)}, u32[]{:S(2)}) collective-permute-start(f32[128,4096]{1,0:T(8,128)S(1)} %get-tuple-element.22), channel_id=1, source_target_pairs={{1,0},{2,1},{3,2},{5,4},{6,5},{7,6},{9,8},{10,9},{11,10},{13,12},{... | collective-permute-start | bytes 6291464 | tf_op jit(solution)/shard_map/ppermute | solution.py:31
  9.4 43.5 %copy-start.6 = (bf16[2,128,4096]{2,1,0:T(8,128)(2,1)S(1)}, bf16[2,128,4096]{2,1,0:T(8,128)(2,1)}, u32[]{:S(2)}) copy-start(bf16[2,128,4096]{2,1,0:T(8,128)(2,1)} %param.12) | copy-start | bytes 6291460
  9.4 43.5 %copy-start.8 = (f32[128,4096]{1,0:T(8,128)S(1)}, f32[128,4096]{1,0:T(8,128)}, u32[]{:S(2)}) copy-start(f32[128,4096]{1,0:T(8,128)} %param.13) | copy-start | bytes 6291460
  59.7 4.4 %collective-permute-start.1 = (f32[3,2,1,4096]{3,2,1,0:T(1,128)S(1)}, f32[3,2,1,4096]{3,2,1,0:T(1,128)S(1)}, u32[]{:S(2)}, u32[]{:S(2)}) collective-permute-start(f32[3,2,1,4096]{3,2,1,0:T(1,128)S(1)} %get-tuple-element.39), channel_id=1, source_target_pairs={{4,0},{8,4},{12,8},{16,12},{20,16},{24,20},{28,24},{5,1},{9,5},{13... | collective-permute-start | bytes 294920 | tf_op jit(solution)/shard_map/ppermute | solution.py:23
  61.6 6.8 %collective-permute-start = (f32[3,2,1,4096]{3,2,1,0:T(1,128)S(1)}, f32[3,2,1,4096]{3,2,1,0:T(1,128)S(1)}, u32[]{:S(2)}, u32[]{:S(2)}) collective-permute-start(f32[3,2,1,4096]{3,2,1,0:T(1,128)S(1)} %get-tuple-element.40), channel_id=1, source_target_pairs={{0,4},{4,8},{8,12},{12,16},{16,20},{20,24},{24,28},{1,5},{5,9},{9,... | collective-permute-start | bytes 294920 | tf_op jit(solution)/shard_map/ppermute | solution.py:20
  68.5 8.5 %copy-start.1 = (f32[2,128,4096]{2,1,0:T(8,128)S(1)}, f32[2,128,4096]{2,1,0:T(8,128)}, u32[]{:S(2)}) copy-start(f32[2,128,4096]{2,1,0:T(8,128)} %param.10) | copy-start | bytes 12582916
  77.5 48.8 %copy-start.12 = (s32[128,4096]{1,0:T(8,128)S(1)}, s32[128,4096]{1,0:T(8,128)}, u32[]{:S(2)}) copy-start(s32[128,4096]{1,0:T(8,128)} %param.17) | copy-start | bytes 6291460
  77.5 45.9 %collective-permute-start.3 = (f32[128,4096]{1,0:T(8,128)S(1)}, f32[128,4096]{1,0:T(8,128)S(1)}, u32[]{:S(2)}, u32[]{:S(2)}) collective-permute-start(f32[128,4096]{1,0:T(8,128)S(1)} %multiply_subtract_fusion.1), channel_id=1, source_target_pairs={{0,1},{1,0},{2,3},{3,2},{4,5},{5,4},{6,7},{7,6},{8,9},{9,8},{10,11... | collective-permute-start | bytes 6291464 | tf_op jit(solution)/shard_map/ppermute | solution.py:113
  123.7 9.6 %copy-start.7 = (bf16[2,128,4096]{2,1,0:T(8,128)(2,1)S(1)}, bf16[2,128,4096]{2,1,0:T(8,128)(2,1)}, u32[]{:S(2)}) copy-start(bf16[2,128,4096]{2,1,0:T(8,128)(2,1)} %param.12) | copy-start | bytes 6291460
  123.7 90.9 %collective-permute-start.4 = (f32[128,4096]{1,0:T(8,128)S(1)}, f32[128,4096]{1,0:T(8,128)}, u32[]{:S(2)}, u32[]{:S(2)}) collective-permute-start(f32[128,4096]{1,0:T(8,128)S(1)} %add.85), channel_id=1, source_target_pairs={{0,2},{1,3},{2,0},{3,1},{4,6},{5,7},{6,4},{7,5},{8,10},{9,11},{10,... | collective-permute-start | bytes 6291464 | tf_op jit(solution)/shard_map/ppermute | solution.py:113
  126.6 97.3 %collective-permute-start.7 = (f32[1,4096]{1,0:T(1,128)S(1)}, f32[1,4096]{1,0:T(1,128)S(1)}, u32[]{:S(2)}, u32[]{:S(2)}) collective-permute-start(f32[1,4096]{1,0:T(1,128)S(1)} %get-tuple-element.33), channel_id=1, source_target_pairs={{0,4},{4,8},{8,12},{12,16},{16,20},{20,24},{24,28},{1,5},{5,9},{9,... | collective-permute-start | bytes 49160 | tf_op jit(solution)/shard_map/ppermute | solution.py:20
  128.5 86.1 %copy-start.10 = (f32[128,4096]{1,0:T(8,128)S(1)}, f32[128,4096]{1,0:T(8,128)}, u32[]{:S(2)}) copy-start(f32[128,4096]{1,0:T(8,128)} %param.16) | copy-start | bytes 6291460
  128.5 86.1 %copy-start.13 = (f32[128,4096]{1,0:T(8,128)S(1)}, f32[128,4096]{1,0:T(8,128)}, u32[]{:S(2)}) copy-start(f32[128,4096]{1,0:T(8,128)} %param.15) | copy-start | bytes 6291460
  128.5 95.3 %collective-permute-start.8 = (f32[1,4096]{1,0:T(1,128)S(1)}, f32[1,4096]{1,0:T(1,128)S(1)}, u32[]{:S(2)}, u32[]{:S(2)}) collective-permute-start(f32[1,4096]{1,0:T(1,128)S(1)} %get-tuple-element.34), channel_id=1, source_target_pairs={{4,0},{8,4},{12,8},{16,12},{20,16},{24,20},{28,24},{5,1},{9,5},{13... | collective-permute-start | bytes 49160 | tf_op jit(solution)/shard_map/ppermute | solution.py:23
  217.2 7.4 %collective-permute-start.5 = (f32[1,4096]{1,0:T(1,128)S(1)}, f32[1,4096]{1,0:T(1,128)S(1)}, u32[]{:S(2)}, u32[]{:S(2)}) collective-permute-start(f32[1,4096]{1,0:T(1,128)S(1)} %get-tuple-element.35), channel_id=1, source_target_pairs={{0,4},{4,8},{8,12},{12,16},{16,20},{20,24},{24,28},{1,5},{5,9},{9,... | collective-permute-start | bytes 49160 | tf_op jit(solution)/shard_map/ppermute | solution.py:20
  219.1 6.0 %collective-permute-start.6 = (f32[1,4096]{1,0:T(1,128)S(1)}, f32[1,4096]{1,0:T(1,128)S(1)}, u32[]{:S(2)}, u32[]{:S(2)}) collective-permute-start(f32[1,4096]{1,0:T(1,128)S(1)} %get-tuple-element.36), channel_id=1, source_target_pairs={{4,0},{8,4},{12,8},{16,12},{20,16},{24,20},{28,24},{5,1},{9,5},{13... | collective-permute-start | bytes 49160 | tf_op jit(solution)/shard_map/ppermute | solution.py:23
  229.8 9.4 %collective-permute-start.10 = (f32[1,4096]{1,0:T(1,128)S(1)}, f32[1,4096]{1,0:T(1,128)S(1)}, u32[]{:S(2)}, u32[]{:S(2)}) collective-permute-start(f32[1,4096]{1,0:T(1,128)S(1)} %get-tuple-element.32), channel_id=1, source_target_pairs={{4,0},{8,4},{12,8},{16,12},{20,16},{24,20},{28,24},{5,1},{9,5},{13... | collective-permute-start | bytes 49160 | tf_op jit(solution)/shard_map/ppermute | solution.py:23
  234.3 6.0 %collective-permute-start.9 = (f32[1,4096]{1,0:T(1,128)S(1)}, f32[1,4096]{1,0:T(1,128)S(1)}, u32[]{:S(2)}, u32[]{:S(2)}) collective-permute-start(f32[1,4096]{1,0:T(1,128)S(1)} %get-tuple-element.31), channel_id=1, source_target_pairs={{0,4},{4,8},{8,12},{12,16},{16,20},{20,24},{24,28},{1,5},{5,9},{9,... | collective-permute-start | bytes 49160 | tf_op jit(solution)/shard_map/ppermute | solution.py:20
  243.1 8.7 %copy-start.2 = (f32[2,128,4096]{2,1,0:T(8,128)S(1)}, f32[2,128,4096]{2,1,0:T(8,128)}, u32[]{:S(2)}) copy-start(f32[2,128,4096]{2,1,0:T(8,128)} %get-tuple-element.20) | copy-start | bytes 12582916
  245.0 9.0 %collective-permute-start.11 = (f32[1,4096]{1,0:T(1,128)S(1)}, f32[1,4096]{1,0:T(1,128)S(1)}, u32[]{:S(2)}, u32[]{:S(2)}) collective-permute-start(f32[1,4096]{1,0:T(1,128)S(1)} %get-tuple-element.29), channel_id=1, source_target_pairs={{0,4},{4,8},{8,12},{12,16},{16,20},{20,24},{24,28},{1,5},{5,9},{9,... | collective-permute-start | bytes 49160 | tf_op jit(solution)/shard_map/ppermute | solution.py:20
  247.0 7.1 %collective-permute-start.12 = (f32[1,4096]{1,0:T(1,128)S(1)}, f32[1,4096]{1,0:T(1,128)S(1)}, u32[]{:S(2)}, u32[]{:S(2)}) collective-permute-start(f32[1,4096]{1,0:T(1,128)S(1)} %get-tuple-element.30), channel_id=1, source_target_pairs={{4,0},{8,4},{12,8},{16,12},{20,16},{24,20},{28,24},{5,1},{9,5},{13... | collective-permute-start | bytes 49160 | tf_op jit(solution)/shard_map/ppermute | solution.py:23
  258.7 9.6 %copy-start.3 = (f32[128,4096]{1,0:T(8,128)}, f32[128,4096]{1,0:T(8,128)S(1)}, u32[]{:S(2)}) copy-start(f32[128,4096]{1,0:T(8,128)S(1)} %slice_add_fusion.2) | copy-start | bytes 6291460
  258.7 8.8 %collective-permute-start.13 = (f32[1,4096]{1,0:T(1,128)S(1)}, f32[1,4096]{1,0:T(1,128)S(1)}, u32[]{:S(2)}, u32[]{:S(2)}) collective-permute-start(f32[1,4096]{1,0:T(1,128)S(1)} %get-tuple-element.27), channel_id=1, source_target_pairs={{0,4},{4,8},{8,12},{12,16},{16,20},{20,24},{24,28},{1,5},{5,9},{9,... | collective-permute-start | bytes 49160 | tf_op jit(solution)/shard_map/ppermute | solution.py:20
  260.7 6.9 %collective-permute-start.14 = (f32[1,4096]{1,0:T(1,128)S(1)}, f32[1,4096]{1,0:T(1,128)S(1)}, u32[]{:S(2)}, u32[]{:S(2)}) collective-permute-start(f32[1,4096]{1,0:T(1,128)S(1)} %get-tuple-element.28), channel_id=1, source_target_pairs={{4,0},{8,4},{12,8},{16,12},{20,16},{24,20},{28,24},{5,1},{9,5},{13... | collective-permute-start | bytes 49160 | tf_op jit(solution)/shard_map/ppermute | solution.py:23
  (5 other events, 23.9 us)
